TPU v7x, 512 devices: a whole 4x8x8 slice. The times are simulated.
512 devices in a mesh: subj: 16 (over y_lo, x), depth: 32 (over y_hi, z, core).
Axes of the slice: x: 4, y: 8 (y_hi: 2, y_lo: 4; y = y_hi * 4 + y_lo), z: 8, core: 2. Of those that a mesh axis runs over, the one named last changes fastest.
Arguments:
- images: float32 [16, 160, 128, 128], P('subj', 'depth'), may hold values from -6 to 6
- velocity: float32 [3, 16, 160, 128, 128], P(None, 'subj', 'depth'), may hold values from -3 to 3
- ref_index: int32 [4], replicated, may hold values from 0 to 15
- ref_weights: int32 [16, 4], P('subj'), may hold values from 0 to 16
Outputs:
- velocity_out: float32 [3, 16, 160, 128, 128], P(None, 'subj', 'depth')
Inputs may be any that keep to these rules, and one draw needn't show every extreme that they name: `ref_index`: subject indices of the references; they may repeat. `ref_weights`: numerators over 16.
All inputs are finite; a program needn't handle non-finite values.
Results may differ from a plain program's by a relative error of at most 0.0003.
Values sent between devices are 32-bit elements; how exact they have to be, the bound alone decides.
A program may use at most 64 MiB of HBM per device.

v0:
```python
import math
import jax
import jax.numpy as jnp
from jax import lax
from jax.sharding import PartitionSpec as P

X = 128
Y = 128
ZD = 5
SUBJ_DEV = 1
NREF = 4
WIN = 9
RG = 3
WDEN = 16


def padded(shard, sides, width):
    for axis, dim in sides:
        devices, length = (lax.axis_size(axis), shard.shape[dim])
        up = [(i, (i + 1) % devices) for i in range(devices - 1)]
        down = [(j, i) for i, j in up]
        last = lax.slice_in_dim(shard, length - width, length, axis=dim)
        first = lax.slice_in_dim(shard, 0, width, axis=dim)
        before = lax.ppermute(last, axis, up)
        after = lax.ppermute(first, axis, down)
        shard = jnp.concatenate([before, shard, after], axis=dim)
    return shard


def spread(shard, axis, root):
    mine = lax.axis_index(axis) == root
    return lax.psum(jnp.where(mine, shard, jnp.zeros_like(shard)), axis)


def gauss_taps():
    raw = [math.exp(-0.5 * offset * offset) for offset in range(-RG, RG + 1)]
    total = sum(raw)
    return [value / total for value in raw]


def band_matrix(length, taps):
    radius = len(taps) // 2
    rows_idx = lax.broadcasted_iota(jnp.int32, (length, length), 0)
    cols_idx = lax.broadcasted_iota(jnp.int32, (length, length), 1)
    matrix = jnp.zeros((length, length), jnp.float32)
    for offset in range(len(taps)):
        matrix = matrix + jnp.where(rows_idx - cols_idx == offset - radius, taps[offset], 0.0)
    return matrix


def planes_xy(field, matrix_x, matrix_y):
    across = jnp.dot(field, matrix_y, precision=lax.Precision.HIGHEST)
    return jnp.einsum("wx,pxy->pwy", matrix_x, across, precision=lax.Precision.HIGHEST)


def depth_window(field, taps, planes, axis):
    total = taps[0] * lax.slice_in_dim(field, 0, planes, axis=axis)
    for offset in range(1, len(taps)):
        total = total + taps[offset] * lax.slice_in_dim(field, offset, offset + planes, axis=axis)
    return total


def boxed(field, box_x, box_y):
    summed = depth_window(field, [1.0] * WIN, ZD, 0)
    return planes_xy(summed, box_x, box_y) / float(WIN**3)


def local_slab(images, which):
    slot_idx = which % SUBJ_DEV
    return lax.dynamic_index_in_dim(images, slot_idx, 0, keepdims=False)


def on_device(images, velocity, ref_index, ref_weights):
    radius = WIN // 2
    ones_taps = [1.0] * WIN
    box_x = band_matrix(X, ones_taps)
    box_y = band_matrix(Y, ones_taps)
    taps = gauss_taps()
    smooth_x = band_matrix(X, taps)
    smooth_y = band_matrix(Y, taps)
    own_ext = padded(images, (("depth", 1),), radius + 1)
    sent = []
    for refnum in range(NREF):
        which = ref_index[refnum]
        sent.append(spread(local_slab(images, which), "subj", which // SUBJ_DEV))
    ref_ext = padded(jnp.stack(sent), (("depth", 1),), radius)
    moving_ext = own_ext[0]
    inner = moving_ext[1:-1]
    core = moving_ext[radius + 1 : radius + 1 + ZD]
    mean_i = boxed(inner, box_x, box_y)
    var_i = boxed(inner * inner, box_x, box_y) - mean_i * mean_i + 1e-05
    coeffs = jnp.zeros_like(core)
    for refnum in range(NREF):
        fixed_ext = ref_ext[refnum]
        fixed_core = fixed_ext[radius : radius + ZD]
        mean_j = boxed(fixed_ext, box_x, box_y)
        var_j = boxed(fixed_ext * fixed_ext, box_x, box_y) - mean_j * mean_j + 1e-05
        covariance = boxed(inner * fixed_ext, box_x, box_y) - mean_i * mean_j
        term = (
            2.0
            * covariance
            / (var_i * var_j)
            * (fixed_core - mean_j - covariance / var_i * (core - mean_i))
        )
        coeffs = coeffs + ref_weights[0, refnum].astype(jnp.float32) / float(WDEN) * term
    grad_depth = (moving_ext[radius + 2 : radius + 2 + ZD] - moving_ext[radius : radius + ZD]) * 0.5
    pad_x = jnp.pad(core, ((0, 0), (1, 1), (0, 0)))
    grad_x = (pad_x[:, 2:, :] - pad_x[:, :-2, :]) * 0.5
    pad_y = jnp.pad(core, ((0, 0), (0, 0), (1, 1)))
    grad_y = (pad_y[:, :, 2:] - pad_y[:, :, :-2]) * 0.5
    forces = [jnp.stack([coeffs * grad_depth, coeffs * grad_x, coeffs * grad_y])]
    force_all = jnp.stack(forces, axis=1)
    force_ext = padded(force_all, (("depth", 2),), RG)
    summed = depth_window(force_ext, taps, ZD, 2)
    flat = summed.reshape((3 * SUBJ_DEV * ZD, X, Y))
    smooth = planes_xy(flat, smooth_x, smooth_y).reshape((3, SUBJ_DEV, ZD, X, Y))
    return velocity + 40.0 * smooth


def solution(mesh):
    placed = (
        P("subj", "depth", None, None),
        P(None, "subj", "depth", None, None),
        P(),
        P("subj", None),
    )
    return jax.shard_map(
        on_device,
        mesh=mesh,
        in_specs=placed,
        out_specs=P(None, "subj", "depth", None, None),
        check_vma=False,
    )
```

profile of v0, /device:TPU:48, one launch (start us, length us, event | category | flops | bytes accessed | tf_op | source)
XLA Modules:
  0.0 281.9 jit_solution(16324112334780596169)
XLA Ops:
  6.5 1.1 copy.5
  7.7 11.7 %collective-permute-start.1 = (f32[1,5,128,128]{2,3,1,0:T(8,128)S(1)}, f32[1,5,128,128]{2,3,1,0:T(8,128)S(1)}, u32[]{:S(2)}, u32[]{:S(2)}) collective-permute-start(f32[1,5,128,128]{2,3,1,0:T(8,128)S(1)} %copy.5), channel_id=1, source_target_pairs={{1,0},{2,1},{3,2},{4,3},{5,4},{6,5},{7,6},{8,7},{9,8},{10,9},{11,1... | collective-permute-start | bytes 983048 | tf_op jit(solution)/shard_map/ppermute | solution.py:25
  19.4 1.9 collective-permute-start
  21.3 1.5 fusion.573
  25.3 1.9 collective-permute-done.1
  27.3 9.8 %collective-permute-done = f32[1,5,128,128]{2,3,1,0:T(8,128)S(1)} collective-permute-done((f32[1,5,128,128]{2,3,1,0:T(8,128)S(1)}, f32[1,5,128,128]{2,3,1,0:T(8,128)S(1)}, u32[]{:S(2)}, u32[]{:S(2)}) %collective-permute-start) | collective-permute-done | bytes 327712 | tf_op jit(solution)/shard_map/ppermute | solution.py:24
  37.1 0.6 fusion.73
  37.7 1.5 bitcast_subtract_fusion
  39.2 155.9 %all-reduce.5.cloned.1.call-done = (f32[5,128,128]{1,2,0:T(8,128)}, f32[5,128,128]{1,2,0:T(8,128)}, f32[5,128,128]{1,2,0:T(8,128)}, f32[5,128,128]{1,2,0:T(8,128)}) async-done(((f32[5,128,128]{1,2,0:T(8,128)}, f32[5,128,128]{1,2,0:T(8,128)}, f32[5,128,128]{1,2,0:T(8,128)}, f32[5,128,128]{1,2,0:T(8,128)}), (f32[5,128,128]{1,2,0:T(8,128)}, f32[5,128,128]{1,2,0:T(8,128)}, f32[5,128,128]{1,2,0:T(8,128)}, ...) | async-done | bytes 1310736 | tf_op jit(solution)/shard_map/psum | solution.py:32
  195.1 1.4 pad_maximum_fusion.2
  196.7 1.9 collective-permute-start.2
  198.7 9.7 %collective-permute-start.3 = (f32[4,4,128,128]{2,3,1,0:T(8,128)S(1)}, f32[4,4,128,128]{2,3,1,0:T(8,128)S(1)}, u32[]{:S(2)}, u32[]{:S(2)}) collective-permute-start(f32[4,4,128,128]{2,3,1,0:T(8,128)S(1)} %get-tuple-element.19), channel_id=1, source_target_pairs={{1,0},{2,1},{3,2},{4,3},{5,4},{6,5},{7,6},{8,7},{9,8},{10,9},{11,1... | collective-permute-start | bytes 3145736 | tf_op jit(solution)/shard_map/ppermute | solution.py:25
  208.3 0.7 fusion.572
  211.8 0.6 fusion.161
  212.4 0.5 fusion.23
  212.8 17.3 %collective-permute-done.2 = f32[4,4,128,128]{2,3,1,0:T(8,128)S(1)} collective-permute-done((f32[4,4,128,128]{2,3,1,0:T(8,128)S(1)}, f32[4,4,128,128]{2,3,1,0:T(8,128)S(1)}, u32[]{:S(2)}, u32[]{:S(2)}) %collective-permute-start.2) | collective-permute-done | bytes 1048608 | tf_op jit(solution)/shard_map/ppermute | solution.py:24
  230.1 1.8 collective-permute-done.3
  231.9 0.6 maximum_maximum_fusion
  232.5 0.6 fusion.165
  233.1 0.6 fusion.119
  233.6 0.6 fusion.98
  234.2 0.6 fusion.140
  235.3 0.6 fusion.94
  235.9 1.0 slice_multiply_fusion.7
  236.8 0.6 fusion.186
  237.4 0.6 fusion.111
  238.0 0.6 fusion.132
  238.6 0.6 fusion.153
  239.1 0.6 fusion.157
  239.7 0.6 fusion.136
  240.3 0.6 fusion.115
  241.4 0.5 fusion.7
  241.8 0.5 fusion.12
  242.8 0.5 fusion.22
  243.3 0.5 fusion.9
  243.8 0.5 fusion.4
  244.3 0.5 fusion.14
  244.7 0.6 fusion.41
  245.3 0.9 fusion.46
  246.2 0.6 fusion.36
  246.8 0.8 fusion.567
  247.8 1.9 collective-permute-start.4
  249.7 9.8 %collective-permute-start.5 = (f32[3,1,3,128,128]{3,4,2,1,0:T(8,128)S(1)}, f32[3,1,3,128,128]{3,4,2,1,0:T(8,128)S(1)}, u32[]{:S(2)}, u32[]{:S(2)}) collective-permute-start(f32[3,1,3,128,128]{3,4,2,1,0:T(8,128)S(1)} %get-tuple-element.21), channel_id=1, source_target_pairs={{1,0},{2,1},{3,2},{4,3},{5,4},{6,5},{7,6},{8,7},{9,8},{10,9},{11,1... | collective-permute-start | bytes 1769480 | tf_op jit(solution)/shard_map/ppermute | solution.py:25
  259.6 9.9 %collective-permute-done.4 = f32[3,1,3,128,128]{3,4,2,1,0:T(8,128)S(1)} collective-permute-done((f32[3,1,3,128,128]{3,4,2,1,0:T(8,128)S(1)}, f32[3,1,3,128,128]{3,4,2,1,0:T(8,128)S(1)}, u32[]{:S(2)}, u32[]{:S(2)}) %collective-permute-start.4) | collective-permute-done | bytes 589856 | tf_op jit(solution)/shard_map/ppermute | solution.py:24
  269.4 1.8 collective-permute-done.5
  271.6 1.0 fusion.191
  272.7 1.0 convolution_multiply_fusion
  274.0 1.1 add.1130
  (24 shorter events, 2.7 us)
Async XLA Ops:
  6.5 188.6 %all-reduce.5.cloned.1.call-start = ((), (), s32[]{:S(2)}) async-start(), calls=%async_computation | async-start | bytes 2621440 | tf_op jit(solution)/shard_map/psum | solution.py:32
  7.7 19.6 %collective-permute-start.1 = (f32[1,5,128,128]{2,3,1,0:T(8,128)S(1)}, f32[1,5,128,128]{2,3,1,0:T(8,128)S(1)}, u32[]{:S(2)}, u32[]{:S(2)}) collective-permute-start(f32[1,5,128,128]{2,3,1,0:T(8,128)S(1)} %copy.5), channel_id=1, source_target_pairs={{1,0},{2,1},{3,2},{4,3},{5,4},{6,5},{7,6},{8,7},{9,8},{10,9},{11,1... | collective-permute-start | bytes 983048 | tf_op jit(solution)/shard_map/ppermute | solution.py:25
  19.4 17.7 %collective-permute-start = (f32[1,5,128,128]{2,3,1,0:T(8,128)S(1)}, f32[1,5,128,128]{2,3,1,0:T(8,128)S(1)}, u32[]{:S(2)}, u32[]{:S(2)}) collective-permute-start(f32[1,5,128,128]{2,3,1,0:T(8,128)S(1)} %copy.5), channel_id=1, source_target_pairs={{0,1},{1,2},{2,3},{3,4},{4,5},{5,6},{6,7},{7,8},{8,9},{9,10},{10,1... | collective-permute-start | bytes 983048 | tf_op jit(solution)/shard_map/ppermute | solution.py:24
  196.5 11.8 %copy-start.5 = (s32[1,4]{1,0:T(1,128)S(1)}, s32[1,4]{1,0:T(1,128)}, u32[]{:S(2)}) copy-start(s32[1,4]{1,0:T(1,128)} %param.7) | copy-start | bytes 52
  196.7 33.4 %collective-permute-start.2 = (f32[4,4,128,128]{2,3,1,0:T(8,128)S(1)}, f32[4,4,128,128]{2,3,1,0:T(8,128)S(1)}, u32[]{:S(2)}, u32[]{:S(2)}) collective-permute-start(f32[4,4,128,128]{2,3,1,0:T(8,128)S(1)} %get-tuple-element.18), channel_id=1, source_target_pairs={{0,1},{1,2},{2,3},{3,4},{4,5},{5,6},{6,7},{7,8},{8,9},{9,10},{10,1... | collective-permute-start | bytes 3145736 | tf_op jit(solution)/shard_map/ppermute | solution.py:24
  198.7 33.2 %collective-permute-start.3 = (f32[4,4,128,128]{2,3,1,0:T(8,128)S(1)}, f32[4,4,128,128]{2,3,1,0:T(8,128)S(1)}, u32[]{:S(2)}, u32[]{:S(2)}) collective-permute-start(f32[4,4,128,128]{2,3,1,0:T(8,128)S(1)} %get-tuple-element.19), channel_id=1, source_target_pairs={{1,0},{2,1},{3,2},{4,3},{5,4},{6,5},{7,6},{8,7},{9,8},{10,9},{11,1... | collective-permute-start | bytes 3145736 | tf_op jit(solution)/shard_map/ppermute | solution.py:25
  209.0 22.9 %copy-start = (f32[5,128,128]{1,2,0:T(8,128)S(1)}, f32[5,128,128]{1,2,0:T(8,128)}, u32[]{:S(2)}) copy-start(f32[5,128,128]{1,2,0:T(8,128)} %get-tuple-element.8) | copy-start | bytes 983044
  209.0 22.9 %copy-start.1 = (f32[5,128,128]{1,2,0:T(8,128)S(1)}, f32[5,128,128]{1,2,0:T(8,128)}, u32[]{:S(2)}) copy-start(f32[5,128,128]{1,2,0:T(8,128)} %get-tuple-element.7) | copy-start | bytes 983044
  209.0 22.9 %copy-start.2 = (f32[5,128,128]{1,2,0:T(8,128)S(1)}, f32[5,128,128]{1,2,0:T(8,128)}, u32[]{:S(2)}) copy-start(f32[5,128,128]{1,2,0:T(8,128)} %get-tuple-element.5) | copy-start | bytes 983044
  209.0 22.9 %copy-start.3 = (f32[5,128,128]{1,2,0:T(8,128)S(1)}, f32[5,128,128]{1,2,0:T(8,128)}, u32[]{:S(2)}) copy-start(f32[5,128,128]{1,2,0:T(8,128)} %get-tuple-element.6) | copy-start | bytes 983044
  247.8 21.6 %collective-permute-start.4 = (f32[3,1,3,128,128]{3,4,2,1,0:T(8,128)S(1)}, f32[3,1,3,128,128]{3,4,2,1,0:T(8,128)S(1)}, u32[]{:S(2)}, u32[]{:S(2)}) collective-permute-start(f32[3,1,3,128,128]{3,4,2,1,0:T(8,128)S(1)} %get-tuple-element.20), channel_id=1, source_target_pairs={{0,1},{1,2},{2,3},{3,4},{4,5},{5,6},{6,7},{7,8},{8,9},{9,10},{10,1... | collective-permute-start | bytes 1769480 | tf_op jit(solution)/shard_map/ppermute | solution.py:24
  249.7 21.5 %collective-permute-start.5 = (f32[3,1,3,128,128]{3,4,2,1,0:T(8,128)S(1)}, f32[3,1,3,128,128]{3,4,2,1,0:T(8,128)S(1)}, u32[]{:S(2)}, u32[]{:S(2)}) collective-permute-start(f32[3,1,3,128,128]{3,4,2,1,0:T(8,128)S(1)} %get-tuple-element.21), channel_id=1, source_target_pairs={{1,0},{2,1},{3,2},{4,3},{5,4},{6,5},{7,6},{8,7},{9,8},{10,9},{11,1... | collective-permute-start | bytes 1769480 | tf_op jit(solution)/shard_map/ppermute | solution.py:25
  272.7 1.3 copy-start.4
Sparse Core Ops, SparseCore 0:
  39.3 155.7 all-reduce.4
where the time goes:
time: 282 us
  waiting for transfers between devices  198 us (70%)
  starting transfers between devices  37 us (13%)
  between operations  19 us (7%)
  matrix products  18.6 us (7%)
  other arithmetic  4.97 us (2%)
  local copies, waits for them, and re-layouts  3.94 us (1%)
    psum x1, waiting for transfers between devices, spread(): return lax.psum(jnp.where(mine, shard, jnp.zeros_like(shard)), axis)  156 us
    ppermute x3, waiting for transfers between devices, padded(): before = lax.ppermute(last, axis, up)  36.9 us
    ppermute x3, starting transfers between devices, padded(): after = lax.ppermute(first, axis, down)  31.2 us
    dot_general x15, matrix products, planes_xy(): jnp.einsum('wx,pxy->pwy', matrix_x, across, precision=lax.Precision.HIGHEST)  9.56 us
    dot_general x15, matrix products, planes_xy(): across = jnp.dot(field, matrix_y, precision=lax.Precision.HIGHEST)  9.09 us
    ppermute x3, starting transfers between devices, padded(): before = lax.ppermute(last, axis, up)  5.76 us
  transfers between devices with their start and end apart: 7, of which 7 were waited for; matrix products, arithmetic and copies ran while one was open for 1% of the time, Pallas kernels for 0%

commit v1 on v0

--- a/solution.py
+++ b/solution.py
@@ -29,7 +29,7 @@
 
 def spread(shard, axis, root):
     mine = lax.axis_index(axis) == root
-    return lax.psum(jnp.where(mine, shard, jnp.zeros_like(shard)), axis)
+    return jnp.sum(lax.all_gather(jnp.where(mine, shard, jnp.zeros_like(shard)), axis), axis=0)
 
 
 def gauss_taps():

time: 282 us -> 468 us (1.66)
  waiting for transfers between devices: 198 us -> 374 us
  other arithmetic: 4.97 us -> 16.8 us
    all_gather x0 -> x4, waiting for transfers between devices: none -> 339 us  [spread(): lax.all_gather(jnp.where(mine, shard, jnp.zeros_like(shard)), axis)]
    psum x1 -> x0, waiting for transfers between devices: 156 us -> none  [spread(): return lax.psum(jnp.where(mine, shard, jnp.zeros_like(shard)), axis)]
    reduce_sum x0 -> x4, other arithmetic: none -> 11.1 us  [spread(): jnp.sum(lax.all_gather(jnp.where(mine, shard, jnp.zeros_like(shard)), axi...]
    ppermute x3, waiting for transfers between devices: 36.9 us -> 29.6 us  [padded(): before = lax.ppermute(last, axis, up)]
  transfers between devices with their start and end apart: 7 -> 10, of which waited for: 7 -> 8; matrix products, arithmetic and copies ran while one was open for 1% -> 3% of each run, Pallas kernels for 0% -> 0%
where the time goes in v1:
time: 468 us
  waiting for transfers between devices  374 us (80%)
  starting transfers between devices  37.1 us (8%)
  between operations  18.6 us (4%)
  matrix products  17.7 us (4%)
  other arithmetic  16.8 us (4%)
    all_gather x4, waiting for transfers between devices, spread(): lax.all_gather(jnp.where(mine, shard, jnp.zeros_like(shard)), axis)  339 us
    ppermute x3, starting transfers between devices, padded(): after = lax.ppermute(first, axis, down)  31.2 us
    ppermute x3, waiting for transfers between devices, padded(): before = lax.ppermute(last, axis, up)  29.6 us
    reduce_sum x4, other arithmetic, spread(): jnp.sum(lax.all_gather(jnp.where(mine, shard, jnp.zeros_like(shard)), axi...  11.1 us
  transfers between devices with their start and end apart: 10, of which 8 were waited for; matrix products, arithmetic and copies ran while one was open for 3% of the time, Pallas kernels for 0%

profile of v1, /device:TPU:48, one launch (start us, length us, event | category | flops | bytes accessed | tf_op | source)
XLA Modules:
  0.0 467.6 jit_solution(1799724147029297153)
XLA Ops:
  6.5 1.5 fusion.573
  10.6 2.1 broadcast_select_fusion.3
  12.7 0.7 all-gather.9.cloned.1.call-update
  13.5 0.7 all-gather.11.cloned.1.call-update
  14.2 0.5 all-gather.7.cloned.1.call-update
  14.9 11.7 %collective-permute-start.1 = (f32[1,5,128,128]{2,3,1,0:T(8,128)S(1)}, f32[1,5,128,128]{2,3,1,0:T(8,128)S(1)}, u32[]{:S(2)}, u32[]{:S(2)}) collective-permute-start(f32[1,5,128,128]{2,3,1,0:T(8,128)S(1)} %copy.12), channel_id=1, source_target_pairs={{1,0},{2,1},{3,2},{4,3},{5,4},{6,5},{7,6},{8,7},{9,8},{10,9},{11,1... | collective-permute-start | bytes 983048 | tf_op jit(solution)/shard_map/ppermute | solution.py:25
  26.7 1.9 collective-permute-start
  28.6 0.7 fusion.572
  31.7 69.5 %all-gather.5.cloned.1.call-done = f32[16,5,128,128]{3,2,1,0:T(8,128)} async-done(((f32[1,5,128,128]{3,2,1,0:T(8,128)}), f32[16,5,128,128]{3,2,1,0:T(8,128)}) %all-gather.5.cloned.1.call-update) | async-done | bytes 5242896 | tf_op jit(solution)/shard_map/all_gather | solution.py:32
  101.2 2.8 reduce_sum.36
  104.2 89.7 %all-gather.9.cloned.1.call-done = f32[16,5,128,128]{3,2,1,0:T(8,128)} async-done(((f32[1,5,128,128]{3,2,1,0:T(8,128)}), f32[16,5,128,128]{3,2,1,0:T(8,128)}) %all-gather.9.cloned.1.call-update) | async-done | bytes 5242896 | tf_op jit(solution)/shard_map/all_gather | solution.py:32
  193.9 2.8 reduce_sum.38
  196.9 90.0 %all-gather.11.cloned.1.call-done = f32[16,5,128,128]{3,2,1,0:T(8,128)} async-done(((f32[1,5,128,128]{3,2,1,0:T(8,128)}), f32[16,5,128,128]{3,2,1,0:T(8,128)}) %all-gather.11.cloned.1.call-update) | async-done | bytes 5242896 | tf_op jit(solution)/shard_map/all_gather | solution.py:32
  286.8 2.8 reduce_sum.39
  289.8 89.6 %all-gather.7.cloned.1.call-done = f32[16,5,128,128]{3,2,1,0:T(8,128)} async-done(((f32[1,5,128,128]{3,2,1,0:T(8,128)}), f32[16,5,128,128]{3,2,1,0:T(8,128)}) %all-gather.7.cloned.1.call-update) | async-done | bytes 5242896 | tf_op jit(solution)/shard_map/all_gather | solution.py:32
  379.4 2.8 reduce_sum.37
  382.7 1.9 collective-permute-start.2
  384.6 9.7 %collective-permute-start.3 = (f32[4,4,128,128]{2,3,1,0:T(8,128)S(1)}, f32[4,4,128,128]{2,3,1,0:T(8,128)S(1)}, u32[]{:S(2)}, u32[]{:S(2)}) collective-permute-start(f32[4,4,128,128]{2,3,1,0:T(8,128)S(1)} %get-tuple-element.15), channel_id=1, source_target_pairs={{1,0},{2,1},{3,2},{4,3},{5,4},{6,5},{7,6},{8,7},{9,8},{10,9},{11,1... | collective-permute-start | bytes 3145736 | tf_op jit(solution)/shard_map/ppermute | solution.py:25
  394.4 0.6 fusion.161
  395.0 0.6 fusion.73
  396.5 19.6 %collective-permute-done.2 = f32[4,4,128,128]{2,3,1,0:T(8,128)S(1)} collective-permute-done((f32[4,4,128,128]{2,3,1,0:T(8,128)S(1)}, f32[4,4,128,128]{2,3,1,0:T(8,128)S(1)}, u32[]{:S(2)}, u32[]{:S(2)}) %collective-permute-start.2) | collective-permute-done | bytes 1048608 | tf_op jit(solution)/shard_map/ppermute | solution.py:24
  416.1 1.8 collective-permute-done.3
  417.8 0.6 maximum_maximum_fusion
  418.4 0.6 fusion.165
  419.0 0.6 fusion.119
  419.6 0.6 fusion.98
  420.2 0.6 fusion.140
  421.1 0.6 fusion.94
  421.7 1.0 slice_multiply_fusion.7
  422.7 0.6 fusion.186
  423.3 0.6 fusion.111
  423.9 0.6 fusion.132
  424.4 0.6 fusion.153
  425.0 0.6 fusion.157
  425.6 0.6 fusion.136
  426.2 0.6 fusion.115
  430.1 0.5 fusion.14
  430.6 0.6 fusion.41
  431.2 0.8 fusion.46
  432.1 0.6 fusion.36
  432.7 0.8 fusion.567
  433.7 1.9 collective-permute-start.4
  435.6 9.8 %collective-permute-start.5 = (f32[3,1,3,128,128]{3,4,2,1,0:T(8,128)S(1)}, f32[3,1,3,128,128]{3,4,2,1,0:T(8,128)S(1)}, u32[]{:S(2)}, u32[]{:S(2)}) collective-permute-start(f32[3,1,3,128,128]{3,4,2,1,0:T(8,128)S(1)} %get-tuple-element.17), channel_id=1, source_target_pairs={{1,0},{2,1},{3,2},{4,3},{5,4},{6,5},{7,6},{8,7},{9,8},{10,9},{11,1... | collective-permute-start | bytes 1769480 | tf_op jit(solution)/shard_map/ppermute | solution.py:25
  445.5 10.0 %collective-permute-done.4 = f32[3,1,3,128,128]{3,4,2,1,0:T(8,128)S(1)} collective-permute-done((f32[3,1,3,128,128]{3,4,2,1,0:T(8,128)S(1)}, f32[3,1,3,128,128]{3,4,2,1,0:T(8,128)S(1)}, u32[]{:S(2)}, u32[]{:S(2)}) %collective-permute-start.4) | collective-permute-done | bytes 589856 | tf_op jit(solution)/shard_map/ppermute | solution.py:24
  455.5 1.8 collective-permute-done.5
  457.6 1.0 fusion.191
  458.7 1.0 convolution_multiply_fusion
  460.0 1.1 add.1122
  (36 shorter events, 7.0 us)
Async XLA Ops:
  6.5 8.2 %copy-start = (f32[1,5,128,128]{3,2,1,0:T(8,128)S(1)}, f32[1,5,128,128]{3,2,1,0:T(8,128)}, u32[]{:S(2)}) copy-start(f32[1,5,128,128]{3,2,1,0:T(8,128)} %param.4) | copy-start | bytes 983044
  6.5 22.1 %copy-start.2 = (s32[1,4]{1,0:T(1,128)S(1)}, s32[1,4]{1,0:T(1,128)}, u32[]{:S(2)}) copy-start(s32[1,4]{1,0:T(1,128)} %param.7) | copy-start | bytes 52
  6.5 94.7 %all-gather.5.cloned.1.call-start = ((), (), s32[]{:S(2)}) async-start(), calls=%async_computation | async-start | bytes 5570560 | tf_op jit(solution)/shard_map/all_gather | solution.py:32
  12.7 181.2 %all-gather.9.cloned.1.call-start = ((), (), s32[]{:S(2)}) async-start(), calls=%async_computation.2 | async-start | bytes 5570560 | tf_op jit(solution)/shard_map/all_gather | solution.py:32
  13.4 273.4 %all-gather.11.cloned.1.call-start = ((), (), s32[]{:S(2)}) async-start(), calls=%async_computation.3 | async-start | bytes 5570560 | tf_op jit(solution)/shard_map/all_gather | solution.py:32
  14.2 365.2 %all-gather.7.cloned.1.call-start = ((), (), s32[]{:S(2)}) async-start(), calls=%async_computation.1 | async-start | bytes 5570560 | tf_op jit(solution)/shard_map/all_gather | solution.py:32
  14.9 379.4 %collective-permute-start.1 = (f32[1,5,128,128]{2,3,1,0:T(8,128)S(1)}, f32[1,5,128,128]{2,3,1,0:T(8,128)S(1)}, u32[]{:S(2)}, u32[]{:S(2)}) collective-permute-start(f32[1,5,128,128]{2,3,1,0:T(8,128)S(1)} %copy.12), channel_id=1, source_target_pairs={{1,0},{2,1},{3,2},{4,3},{5,4},{6,5},{7,6},{8,7},{9,8},{10,9},{11,1... | collective-permute-start | bytes 983048 | tf_op jit(solution)/shard_map/ppermute | solution.py:25
  26.7 367.6 %collective-permute-start = (f32[1,5,128,128]{2,3,1,0:T(8,128)S(1)}, f32[1,5,128,128]{2,3,1,0:T(8,128)S(1)}, u32[]{:S(2)}, u32[]{:S(2)}) collective-permute-start(f32[1,5,128,128]{2,3,1,0:T(8,128)S(1)} %copy.12), channel_id=1, source_target_pairs={{0,1},{1,2},{2,3},{3,4},{4,5},{5,6},{6,7},{7,8},{8,9},{9,10},{10,1... | collective-permute-start | bytes 983048 | tf_op jit(solution)/shard_map/ppermute | solution.py:24
  382.7 33.4 %collective-permute-start.2 = (f32[4,4,128,128]{2,3,1,0:T(8,128)S(1)}, f32[4,4,128,128]{2,3,1,0:T(8,128)S(1)}, u32[]{:S(2)}, u32[]{:S(2)}) collective-permute-start(f32[4,4,128,128]{2,3,1,0:T(8,128)S(1)} %get-tuple-element.14), channel_id=1, source_target_pairs={{0,1},{1,2},{2,3},{3,4},{4,5},{5,6},{6,7},{7,8},{8,9},{9,10},{10,1... | collective-permute-start | bytes 3145736 | tf_op jit(solution)/shard_map/ppermute | solution.py:24
  384.6 33.2 %collective-permute-start.3 = (f32[4,4,128,128]{2,3,1,0:T(8,128)S(1)}, f32[4,4,128,128]{2,3,1,0:T(8,128)S(1)}, u32[]{:S(2)}, u32[]{:S(2)}) collective-permute-start(f32[4,4,128,128]{2,3,1,0:T(8,128)S(1)} %get-tuple-element.15), channel_id=1, source_target_pairs={{1,0},{2,1},{3,2},{4,3},{5,4},{6,5},{7,6},{8,7},{9,8},{10,9},{11,1... | collective-permute-start | bytes 3145736 | tf_op jit(solution)/shard_map/ppermute | solution.py:25
  433.7 21.7 %collective-permute-start.4 = (f32[3,1,3,128,128]{3,4,2,1,0:T(8,128)S(1)}, f32[3,1,3,128,128]{3,4,2,1,0:T(8,128)S(1)}, u32[]{:S(2)}, u32[]{:S(2)}) collective-permute-start(f32[3,1,3,128,128]{3,4,2,1,0:T(8,128)S(1)} %get-tuple-element.16), channel_id=1, source_target_pairs={{0,1},{1,2},{2,3},{3,4},{4,5},{5,6},{6,7},{7,8},{8,9},{9,10},{10,1... | collective-permute-start | bytes 1769480 | tf_op jit(solution)/shard_map/ppermute | solution.py:24
  435.6 21.6 %collective-permute-start.5 = (f32[3,1,3,128,128]{3,4,2,1,0:T(8,128)S(1)}, f32[3,1,3,128,128]{3,4,2,1,0:T(8,128)S(1)}, u32[]{:S(2)}, u32[]{:S(2)}) collective-permute-start(f32[3,1,3,128,128]{3,4,2,1,0:T(8,128)S(1)} %get-tuple-element.17), channel_id=1, source_target_pairs={{1,0},{2,1},{3,2},{4,3},{5,4},{6,5},{7,6},{8,7},{9,8},{10,9},{11,1... | collective-permute-start | bytes 1769480 | tf_op jit(solution)/shard_map/ppermute | solution.py:25
  458.7 1.3 copy-start.1
Sparse Core Ops, SparseCore 0:
  12.8 88.3 all-gather.4
  103.3 90.5 all-gather.8
  196.0 90.7 all-gather.10
  288.7 90.5 all-gather.6
